TPU v7x, 256 devices: a whole 4x4x8 slice. The times are simulated.
256 devices in a mesh: row: 4 (over y), col: 16 (over z, core), layer: 4 (over x).
Axes of the slice: x: 4, y: 4, z: 8, core: 2. Of those that a mesh axis runs over, the one named last changes fastest.
Arguments:
- density: float32 [4096, 4096], P('row', 'col'), may hold values from -1 to 1, as said below
- pattern: int32 [64, 64], replicated, may hold values from 0 to 1, as said below
Outputs:
- purified: float32 [4096, 4096], P('row', 'col')
- traces: float32 [2], replicated
Inputs may be any that keep to these rules, and one draw needn't show every extreme that they name: pattern is symmetric and is 1 on the block diagonal and next to it. density is symmetric and zero outside the blocks that pattern keeps.
All inputs are finite; a program needn't handle non-finite values.
Results may differ from a plain program's by a relative error of at most 0.0003.
Values sent between devices are 32-bit elements; how exact they have to be, the bound alone decides.
No kernel may reach another device: no remote copies, remote signals or barrier semaphores. Data moves between devices by JAX's collectives and lax.ppermute only.
A program may use at most 64 MiB of HBM per device.

v0:
```python
import jax
import jax.numpy as jnp
from jax import lax
from jax.sharding import PartitionSpec as P

BS = 64
STEPS = 2
HIGHEST = lax.Precision.HIGHEST


def pick_columns(tile, layer_index, unit_width, layers):
    tile_rows, tile_cols = tile.shape
    shaped = tile.reshape(tile_rows, tile_cols // (layers * unit_width), layers, unit_width)
    picked = lax.dynamic_index_in_dim(shaped, layer_index, 2, keepdims=False)
    return picked.reshape(tile_rows, tile_cols // layers)


def pick_rows(tile, layer_index, unit_width, layers):
    tile_rows, tile_cols = tile.shape
    shaped = tile.reshape(tile_rows // (layers * unit_width), layers, unit_width, tile_cols)
    picked = lax.dynamic_index_in_dim(shaped, layer_index, 1, keepdims=False)
    return picked.reshape(tile_rows // layers, tile_cols)


def reduce_layers(layer_term):
    summed = lax.psum(layer_term, "layer")
    return summed


def right_panel(right, layer_index, unit_width, layers):
    return lax.all_gather(
        pick_rows(right, layer_index, unit_width, layers), "row", axis=0, tiled=True
    )


def folded_product(left, right, layer_index, unit_width, layers, occupied):
    tall_panel = right_panel(right, layer_index, unit_width, layers)
    layer_term = jnp.dot(
        lax.all_gather(
            pick_columns(left, layer_index, unit_width, layers), "col", axis=1, tiled=True
        ),
        tall_panel,
        precision=HIGHEST,
        preferred_element_type=jnp.float32,
    )
    summed = reduce_layers(layer_term)
    return jnp.where(occupied, summed, jnp.zeros_like(summed))


def body(density, pattern):
    tile_rows, tile_cols = density.shape
    layers = lax.axis_size("layer")
    unit_width = tile_cols // (lax.axis_size("row") * layers)
    layer_index = lax.axis_index("layer")
    row_ids = lax.axis_index("row") * tile_rows + jnp.arange(tile_rows, dtype=jnp.int32)
    col_ids = lax.axis_index("col") * tile_cols + jnp.arange(tile_cols, dtype=jnp.int32)
    blocks = jnp.arange(pattern.shape[0], dtype=jnp.int32)
    row_onehot = (row_ids[:, None] // BS == blocks[None, :]).astype(jnp.bfloat16)
    col_onehot = (blocks[:, None] == col_ids[None, :] // BS).astype(jnp.bfloat16)
    row_pattern = jnp.dot(
        row_onehot, pattern.astype(jnp.bfloat16), preferred_element_type=jnp.float32
    )
    occupied = (
        jnp.dot(row_pattern.astype(jnp.bfloat16), col_onehot, preferred_element_type=jnp.float32)
        > 0.5
    )
    on_diag = row_ids[:, None] == col_ids[None, :]
    current = density
    trace_list = []
    for iteration in range(STEPS):
        square = folded_product(current, current, layer_index, unit_width, layers, occupied)
        cube_term = folded_product(current, square, layer_index, unit_width, layers, occupied)
        current = 3.0 * square - 2.0 * cube_term
        diag_part = jnp.sum(jnp.where(on_diag, current, jnp.zeros_like(current)))
        trace_list.append(lax.psum(diag_part, ("row", "col")))
    stacked = jnp.stack(trace_list)
    return (current, stacked)


def solution(mesh):
    placed = (P("row", "col"), P())
    return jax.shard_map(
        body, mesh=mesh, in_specs=placed, out_specs=(P("row", "col"), P()), check_vma=False
    )
```

profile of v0, /device:TPU:2, one launch (start us, length us, event | category | flops | bytes accessed | tf_op | source)
XLA Modules:
  0.0 601.4 jit_solution(12206215405275679510)
XLA Ops:
  7.2 0.0 all-gather.9.cloned.1.call-start
  7.2 1.7 constant_dynamic-slice_fusion.4
  8.9 0.0 all-gather.9.cloned.1.call-update
  8.9 0.0 all-gather.7.cloned.1.call-start
  9.0 1.6 copy.4
  10.6 0.0 copy-start.2
  10.6 0.7 constant_dynamic-slice_fusion.5
  11.3 0.0 all-gather.7.cloned.1.call-update
  11.3 0.0 all-reduce.6.cloned.1.call-start
  11.4 28.0 %all-gather.9.cloned.1.call-done = f32[1024,256]{1,0:T(8,128)} async-done(((f32[256,256]{1,0:T(8,128)}), f32[1024,256]{1,0:T(8,128)}) %all-gather.9.cloned.1.call-update) | async-done | bytes 1048592 | tf_op jit(solution)/shard_map/all_gather | solution.py:31
  39.3 44.9 %all-gather.7.cloned.1.call-done = f32[1024,1024]{0,1:T(8,128)} async-done(((f32[1024,64]{0,1:T(8,128)}), f32[1024,1024]{0,1:T(8,128)}) %all-gather.7.cloned.1.call-update) | async-done | bytes 4194320 | tf_op jit(solution)/shard_map/all_gather | solution.py:39
  84.2 10.1 %fusion.12 = f32[1024,256]{1,0:T(8,128)} fusion(f32[1024,1024]{0,1:T(8,128)} %all-gather.7.cloned.1.call-done, f32[1024,256]{1,0:T(8,128)} %all-gather.9.cloned.1.call-done), kind=kOutput, calls=%fused_computation.36 | convolution fusion | flops 3221225472 | bytes 6291456 | tf_op jit(solution)/shard_map/dot_general | solution.py:38
  94.3 0.0 all-reduce.6.cloned.1.call-update
  94.4 0.0 all-gather.11.cloned.1.call-start
  94.4 48.7 %all-reduce.6.cloned.1.call-done = f32[1024,256]{1,0:T(8,128)} async-done(((f32[1024,256]{1,0:T(8,128)}), f32[1024,256]{1,0:T(8,128)}) %all-reduce.6.cloned.1.call-update) | async-done | bytes 1048592 | tf_op jit(solution)/shard_map/psum | solution.py:26
  143.2 0.0 copy-done.2
  143.2 1.8 broadcast_select_fusion.1
  145.0 0.0 copy-start.1
  145.0 0.7 constant_dynamic-slice_fusion.3
  145.7 0.0 all-gather.11.cloned.1.call-update
  145.7 0.2 all-reduce.8.cloned.1.call-start
  146.0 28.2 %all-gather.11.cloned.1.call-done = f32[1024,256]{1,0:T(8,128)} async-done(((f32[256,256]{1,0:T(8,128)}), f32[1024,256]{1,0:T(8,128)}) %all-gather.11.cloned.1.call-update) | async-done | bytes 1048592 | tf_op jit(solution)/shard_map/all_gather | solution.py:31
  174.1 10.1 %fusion.13 = f32[1024,256]{1,0:T(8,128)} fusion(f32[1024,1024]{0,1:T(8,128)} %all-gather.7.cloned.1.call-done, f32[1024,256]{1,0:T(8,128)} %all-gather.11.cloned.1.call-done), kind=kOutput, calls=%fused_computation.37 | convolution fusion | flops 3221225472 | bytes 6291456 | tf_op jit(solution)/shard_map/dot_general | solution.py:38
  184.2 0.0 all-reduce.8.cloned.1.call-update
  184.3 0.0 all-gather.15.cloned.1.call-start
  184.3 50.6 %all-reduce.8.cloned.1.call-done = f32[1024,256]{1,0:T(8,128)} async-done(((f32[1024,256]{1,0:T(8,128)}), f32[1024,256]{1,0:T(8,128)}) %all-reduce.8.cloned.1.call-update) | async-done | bytes 1048592 | tf_op jit(solution)/shard_map/psum | solution.py:26
  234.9 0.0 copy-done.1
  234.9 1.5 multiply_subtract_fusion.1
  236.3 0.8 constant_dynamic-slice_fusion.1
  237.1 0.0 all-gather.15.cloned.1.call-update
  237.1 0.0 all-gather.13.cloned.1.call-start
  237.2 0.3 copy.5
  237.5 0.7 constant_dynamic-slice_fusion.2
  238.2 0.0 all-gather.13.cloned.1.call-update
  238.2 0.3 all-reduce.10.cloned.1.call-start
  238.5 27.0 %all-gather.15.cloned.1.call-done = f32[1024,256]{1,0:T(8,128)} async-done(((f32[256,256]{1,0:T(8,128)}), f32[1024,256]{1,0:T(8,128)}) %all-gather.15.cloned.1.call-update) | async-done | bytes 1048592 | tf_op jit(solution)/shard_map/all_gather | solution.py:31
  265.5 44.9 %all-gather.13.cloned.1.call-done = f32[1024,1024]{0,1:T(8,128)} async-done(((f32[1024,64]{0,1:T(8,128)}), f32[1024,1024]{0,1:T(8,128)}) %all-gather.13.cloned.1.call-update) | async-done | bytes 4194320 | tf_op jit(solution)/shard_map/all_gather | solution.py:39
  310.4 10.1 %fusion.14 = f32[1024,256]{1,0:T(8,128)} fusion(f32[1024,1024]{0,1:T(8,128)} %all-gather.13.cloned.1.call-done, f32[1024,256]{1,0:T(8,128)} %all-gather.15.cloned.1.call-done), kind=kOutput, calls=%fused_computation.38 | convolution fusion | flops 3221225472 | bytes 6291456 | tf_op jit(solution)/shard_map/dot_general | solution.py:38
  320.5 0.0 all-reduce.10.cloned.1.call-update
  320.5 0.0 all-gather.17.cloned.1.call-start
  320.5 48.8 %all-reduce.10.cloned.1.call-done = f32[1024,256]{1,0:T(8,128)} async-done(((f32[1024,256]{1,0:T(8,128)}), f32[1024,256]{1,0:T(8,128)}) %all-reduce.10.cloned.1.call-update) | async-done | bytes 1048592 | tf_op jit(solution)/shard_map/psum | solution.py:26
  369.3 1.3 broadcast_select_fusion
  370.7 0.0 copy-start
  370.7 0.7 constant_dynamic-slice_fusion
  371.4 0.0 all-gather.17.cloned.1.call-update
  371.4 0.3 all-reduce.12.cloned.1.call-start
  371.8 28.4 %all-gather.17.cloned.1.call-done = f32[1024,256]{1,0:T(8,128)} async-done(((f32[256,256]{1,0:T(8,128)}), f32[1024,256]{1,0:T(8,128)}) %all-gather.17.cloned.1.call-update) | async-done | bytes 1048592 | tf_op jit(solution)/shard_map/all_gather | solution.py:31
  400.1 10.1 %fusion.15 = f32[1024,256]{1,0:T(8,128)} fusion(f32[1024,1024]{0,1:T(8,128)} %all-gather.13.cloned.1.call-done, f32[1024,256]{1,0:T(8,128)} %all-gather.17.cloned.1.call-done), kind=kOutput, calls=%fused_computation.39 | convolution fusion | flops 3221225472 | bytes 6291456 | tf_op jit(solution)/shard_map/dot_general | solution.py:38
  410.2 0.0 all-reduce.12.cloned.1.call-update
  410.3 50.6 %all-reduce.12.cloned.1.call-done = f32[1024,256]{1,0:T(8,128)} async-done(((f32[1024,256]{1,0:T(8,128)}), f32[1024,256]{1,0:T(8,128)}) %all-reduce.12.cloned.1.call-update) | async-done | bytes 1048592 | tf_op jit(solution)/shard_map/psum | solution.py:26
  460.9 0.0 copy-done
  460.9 3.2 fusion
  464.1 128.6 %all-reduce = (f32[1]{0:T(128)}, f32[1]{0:T(128)}) all-reduce(f32[1]{0:T(128)} %bitcast.13, f32[1]{0:T(128)} %bitcast.12), channel_id=1, replica_groups=mesh['row'=4,'col'=16,'layer'=4] {'row','col'}, use_global_device_ids=true, to_apply=%region_7.8 | all-reduce | flops 2 | bytes 16 | tf_op jit(solution)/shard_map/psum | solution.py:75
  592.7 1.8 pad_maximum_fusion
  (4 shorter events, 0.0 us)
Async XLA Ops:
  7.2 32.2 %all-gather.9.cloned.1.call-start = ((), (), s32[]{:S(2)}) async-start(), calls=%async_computation.1 | async-start | bytes 1310720 | tf_op jit(solution)/shard_map/all_gather | solution.py:31
  8.9 75.3 %all-gather.7.cloned.1.call-start = ((), (), s32[]{:S(2)}) async-start(), calls=%async_computation | async-start | bytes 4456448 | tf_op jit(solution)/shard_map/all_gather | solution.py:39
  10.6 132.6 %copy-start.2 = (s32[64,64]{1,0:T(8,128)S(1)}, s32[64,64]{1,0:T(8,128)}, u32[]{:S(2)}) copy-start(s32[64,64]{1,0:T(8,128)} %param.3) | copy-start | bytes 49156
  11.3 131.9 %all-reduce.6.cloned.1.call-start = ((), (), s32[]{:S(2)}) async-start(), calls=%async_computation.2 | async-start | bytes 2097152 | tf_op jit(solution)/shard_map/psum | solution.py:26
  94.4 79.8 %all-gather.11.cloned.1.call-start = ((), (), s32[]{:S(2)}) async-start(), calls=%async_computation.3 | async-start | bytes 1310720 | tf_op jit(solution)/shard_map/all_gather | solution.py:31
  145.0 89.9 %copy-start.1 = (f32[1024,256]{1,0:T(8,128)S(1)}, f32[1024,256]{1,0:T(8,128)}, u32[]{:S(2)}) copy-start(f32[1024,256]{1,0:T(8,128)} %all-reduce.6.cloned.1.call-done) | copy-start | bytes 3145732
  145.7 89.1 %all-reduce.8.cloned.1.call-start = ((), (), s32[]{:S(2)}) async-start(), calls=%async_computation.4 | async-start | bytes 2097152 | tf_op jit(solution)/shard_map/psum | solution.py:26
  184.3 81.2 %all-gather.15.cloned.1.call-start = ((), (), s32[]{:S(2)}) async-start(), calls=%async_computation.6 | async-start | bytes 1310720 | tf_op jit(solution)/shard_map/all_gather | solution.py:31
  237.1 73.2 %all-gather.13.cloned.1.call-start = ((), (), s32[]{:S(2)}) async-start(), calls=%async_computation.5 | async-start | bytes 4456448 | tf_op jit(solution)/shard_map/all_gather | solution.py:39
  238.2 131.1 %all-reduce.10.cloned.1.call-start = ((), (), s32[]{:S(2)}) async-start(), calls=%async_computation.7 | async-start | bytes 2097152 | tf_op jit(solution)/shard_map/psum | solution.py:26
  320.5 79.6 %all-gather.17.cloned.1.call-start = ((), (), s32[]{:S(2)}) async-start(), calls=%async_computation.8 | async-start | bytes 1310720 | tf_op jit(solution)/shard_map/all_gather | solution.py:31
  370.7 90.2 %copy-start = (f32[1024,256]{1,0:T(8,128)S(1)}, f32[1024,256]{1,0:T(8,128)}, u32[]{:S(2)}) copy-start(f32[1024,256]{1,0:T(8,128)} %all-reduce.10.cloned.1.call-done) | copy-start | bytes 3145732
  371.4 89.4 %all-reduce.12.cloned.1.call-start = ((), (), s32[]{:S(2)}) async-start(), calls=%async_computation.9 | async-start | bytes 2097152 | tf_op jit(solution)/shard_map/psum | solution.py:26
Sparse Core Ops, SparseCore 0:
  9.8 29.4 all-gather.8
  41.7 42.4 all-gather.6
  94.5 48.6 all-reduce.5
  145.8 28.2 all-gather.10
  184.4 50.4 all-reduce.7
  237.2 28.2 all-gather.14
  267.9 42.4 all-gather.12
  320.6 48.6 all-reduce.9
  371.9 28.2 all-gather.16
  410.4 50.4 all-reduce.11
where the time goes:
time: 602 us; the launch traced here: 601 us
  waiting for transfers between devices  400 us (66%)
  blocking collectives  129 us (21%)
  matrix products  42.3 us (7%)
  between operations  14.3 us (2%)
  other arithmetic  7.89 us (1%)
  local copies, waits for them, and re-layouts  7.27 us (1%)
    psum x4, waiting for transfers between devices, reduce_layers(): summed = lax.psum(layer_term, 'layer')  199 us
    psum x1, blocking collectives, body(): trace_list.append(lax.psum(diag_part, ('row', 'col')))  129 us
    all_gather x4, waiting for transfers between devices, right_panel(): lax.all_gather(pick_rows(right, layer_index, unit_width, layers), 'row',...  111 us
    all_gather x2, waiting for transfers between devices, folded_product(): lax.all_gather(pick_columns(left, layer_index, unit_width, layers), 'col'...  89.7 us
    dot_general x4, matrix products, folded_product(): jnp.dot(lax.all_gather(pick_columns(left, layer_index, unit_width, layers...  40.5 us
  transfers between devices with their start and end apart: 10, of which 10 were waited for; matrix products, arithmetic and copies ran while one was open for 1% of the time, Pallas kernels for 0%

commit v1 on v0

--- a/solution.py
+++ b/solution.py
@@ -28,8 +28,14 @@
 
 
 def right_panel(right, layer_index, unit_width, layers):
-    return lax.all_gather(
-        pick_rows(right, layer_index, unit_width, layers), "row", axis=0, tiled=True
+    return jnp.concatenate(
+        jax.lax.all_to_all(
+            jnp.stack(jax.lax.psum(1, "row") * [pick_rows(right, layer_index, unit_width, layers)]),
+            "row",
+            0,
+            0,
+        ),
+        axis=0,
     )
 
 

time: 602 us -> 517 us (0.86)
  waiting for transfers between devices: 400 us -> 247 us
  blocking collectives: 129 us -> 202 us
    all_gather x4 -> x0, waiting for transfers between devices: 111 us -> none  [right_panel(): lax.all_gather(pick_rows(right, layer_index, unit_width, layers), 'row',...]
    all_to_all x0 -> x4, blocking collectives: none -> 73.8 us  [right_panel(): jax.lax.all_to_all(jnp.stack(jax.lax.psum(1, 'row') * [pick_rows(right, l...]
    all_gather x2, waiting for transfers between devices: 89.7 us -> 51.6 us  [folded_product(): lax.all_gather(pick_columns(left, layer_index, unit_width, layers), 'col'...]
  transfers between devices with their start and end apart: 10 -> 6, of which waited for: 10 -> 6; matrix products, arithmetic and copies ran while one was open for 1% -> 0% of each run, Pallas kernels for 0% -> 0%
where the time goes in v1:
time: 517 us; the launch traced here: 516 us
  waiting for transfers between devices  247 us (48%)
  blocking collectives  202 us (39%)
  matrix products  39.2 us (8%)
  between operations  14.2 us (3%)
  other arithmetic  8 us (2%)
    psum x4, waiting for transfers between devices, reduce_layers(): summed = lax.psum(layer_term, 'layer')  196 us
    psum x1, blocking collectives, body(): trace_list.append(lax.psum(diag_part, ('row', 'col')))  129 us
    all_to_all x4, blocking collectives, right_panel(): jax.lax.all_to_all(jnp.stack(jax.lax.psum(1, 'row') * [pick_rows(right, l...  73.8 us
    all_gather x2, waiting for transfers between devices, folded_product(): lax.all_gather(pick_columns(left, layer_index, unit_width, layers), 'col'...  51.6 us
    dot_general x4, matrix products, folded_product(): jnp.dot(lax.all_gather(pick_columns(left, layer_index, unit_width, layers...  37.4 us
  transfers between devices with their start and end apart: 6, of which 6 were waited for; matrix products, arithmetic and copies ran while one was open for 0% of the time, Pallas kernels for 0%

profile of v1, /device:TPU:2, one launch (start us, length us, event | category | flops | bytes accessed | tf_op | source)
XLA Modules:
  0.0 516.2 jit_solution(11720555575758756446)
XLA Ops:
  7.2 0.0 all-gather.3.cloned.1.call-start
  7.2 1.6 copy.4
  8.8 0.7 constant_dynamic-slice_fusion.5
  9.5 0.0 all-gather.3.cloned.1.call-update
  9.5 0.0 all-reduce.6.cloned.1.call-start
  9.6 1.0 constant_dynamic-slice_fusion.4
  10.6 0.1 stack.21
  10.7 19.4 %all_to_all.20 = f32[4,256,256]{2,1,0:T(8,128)S(1)} all-to-all(f32[4,256,256]{2,1,0:T(8,128)S(1)} %stack.21), channel_id=1, replica_groups=mesh['row'=4,'col'=16,'layer'=4] {'row'}, dimensions={0} | all-to-all | bytes 2097152 | tf_op jit(solution)/shard_map/all_to_all | solution.py:32
  30.0 0.0 copy-start.3
  30.0 25.7 %all-gather.3.cloned.1.call-done = f32[1024,1024]{0,1:T(8,128)} async-done(((f32[1024,64]{0,1:T(8,128)}), f32[1024,1024]{0,1:T(8,128)}) %all-gather.3.cloned.1.call-update) | async-done | bytes 4194320 | tf_op jit(solution)/shard_map/all_gather | solution.py:45
  55.8 9.8 %fusion.12 = f32[1024,256]{1,0:T(8,128)} fusion(f32[1024,1024]{0,1:T(8,128)} %all-gather.3.cloned.1.call-done, f32[1024,256]{1,0:T(8,128)S(1)} %bitcast.27), kind=kOutput, calls=%fused_computation.36 | convolution fusion | flops 3221225472 | bytes 6291456 | tf_op jit(solution)/shard_map/dot_general | solution.py:44
  65.6 0.0 all-reduce.6.cloned.1.call-update
  65.6 0.0 all-reduce.8.cloned.1.call-start
  65.7 48.5 %all-reduce.6.cloned.1.call-done = f32[1024,256]{1,0:T(8,128)} async-done(((f32[1024,256]{1,0:T(8,128)}), f32[1024,256]{1,0:T(8,128)}) %all-reduce.6.cloned.1.call-update) | async-done | bytes 1048592 | tf_op jit(solution)/shard_map/psum | solution.py:26
  114.2 0.0 copy-done.3
  114.2 1.8 broadcast_select_fusion.1
  116.0 0.1 stack.22
  116.1 18.1 %all_to_all.21 = f32[4,256,256]{2,1,0:T(8,128)S(1)} all-to-all(f32[4,256,256]{2,1,0:T(8,128)S(1)} %stack.22), channel_id=1, replica_groups=mesh['row'=4,'col'=16,'layer'=4] {'row'}, dimensions={0} | all-to-all | bytes 2097152 | tf_op jit(solution)/shard_map/all_to_all | solution.py:32
  134.2 0.0 copy-start.2
  134.2 9.9 %fusion.13 = f32[1024,256]{1,0:T(8,128)} fusion(f32[1024,1024]{0,1:T(8,128)} %all-gather.3.cloned.1.call-done, f32[1024,256]{1,0:T(8,128)S(1)} %bitcast.29), kind=kOutput, calls=%fused_computation.37 | convolution fusion | flops 3221225472 | bytes 6291456 | tf_op jit(solution)/shard_map/dot_general | solution.py:44
  144.1 0.0 all-reduce.8.cloned.1.call-update
  144.2 0.0 all-gather.5.cloned.1.call-start
  144.2 49.4 %all-reduce.8.cloned.1.call-done = f32[1024,256]{1,0:T(8,128)} async-done(((f32[1024,256]{1,0:T(8,128)}), f32[1024,256]{1,0:T(8,128)}) %all-reduce.8.cloned.1.call-update) | async-done | bytes 1048592 | tf_op jit(solution)/shard_map/psum | solution.py:26
  193.6 0.0 copy-done.2
  193.6 1.5 multiply_subtract_fusion.1
  195.0 0.3 copy.5
  195.4 0.7 constant_dynamic-slice_fusion.2
  196.1 0.0 all-gather.5.cloned.1.call-update
  196.1 0.0 all-reduce.10.cloned.1.call-start
  196.2 0.1 stack.23
  196.3 18.1 %all_to_all.22 = f32[4,256,256]{2,1,0:T(8,128)S(1)} all-to-all(f32[4,256,256]{2,1,0:T(8,128)S(1)} %stack.23), channel_id=1, replica_groups=mesh['row'=4,'col'=16,'layer'=4] {'row'}, dimensions={0} | all-to-all | bytes 2097152 | tf_op jit(solution)/shard_map/all_to_all | solution.py:32
  214.4 25.9 %all-gather.5.cloned.1.call-done = f32[1024,1024]{0,1:T(8,128)} async-done(((f32[1024,64]{0,1:T(8,128)}), f32[1024,1024]{0,1:T(8,128)}) %all-gather.5.cloned.1.call-update) | async-done | bytes 4194320 | tf_op jit(solution)/shard_map/all_gather | solution.py:45
  240.3 9.8 %fusion.14 = f32[1024,256]{1,0:T(8,128)} fusion(f32[1024,1024]{0,1:T(8,128)} %all-gather.5.cloned.1.call-done, f32[1024,256]{1,0:T(8,128)S(1)} %bitcast.28), kind=kOutput, calls=%fused_computation.38 | convolution fusion | flops 3221225472 | bytes 6291456 | tf_op jit(solution)/shard_map/dot_general | solution.py:44
  250.2 0.0 all-reduce.10.cloned.1.call-update
  250.2 0.0 all-reduce.12.cloned.1.call-start
  250.2 48.5 %all-reduce.10.cloned.1.call-done = f32[1024,256]{1,0:T(8,128)} async-done(((f32[1024,256]{1,0:T(8,128)}), f32[1024,256]{1,0:T(8,128)}) %all-reduce.10.cloned.1.call-update) | async-done | bytes 1048592 | tf_op jit(solution)/shard_map/psum | solution.py:26
  298.8 0.0 copy-start
  298.8 1.5 broadcast_select_fusion
  300.3 0.1 stack.24
  300.4 18.1 %all_to_all.23 = f32[4,256,256]{2,1,0:T(8,128)S(1)} all-to-all(f32[4,256,256]{2,1,0:T(8,128)S(1)} %stack.24), channel_id=1, replica_groups=mesh['row'=4,'col'=16,'layer'=4] {'row'}, dimensions={0} | all-to-all | bytes 2097152 | tf_op jit(solution)/shard_map/all_to_all | solution.py:32
  318.5 0.0 copy-start.1
  318.5 0.0 copy-done
  318.5 7.8 %fusion.15 = f32[1024,256]{1,0:T(8,128)} fusion(f32[1024,1024]{0,1:T(8,128)S(1)} %copy-done, f32[1024,256]{1,0:T(8,128)S(1)} %bitcast.30), kind=kOutput, calls=%fused_computation.39 | convolution fusion | flops 3221225472 | bytes 6291456 | tf_op jit(solution)/shard_map/dot_general | solution.py:44
  326.4 0.0 all-reduce.12.cloned.1.call-update
  326.4 49.4 %all-reduce.12.cloned.1.call-done = f32[1024,256]{1,0:T(8,128)} async-done(((f32[1024,256]{1,0:T(8,128)}), f32[1024,256]{1,0:T(8,128)}) %all-reduce.12.cloned.1.call-update) | async-done | bytes 1048592 | tf_op jit(solution)/shard_map/psum | solution.py:26
  375.8 0.0 copy-done.1
  375.8 3.2 fusion
  379.0 128.6 %all-reduce = (f32[1]{0:T(128)}, f32[1]{0:T(128)}) all-reduce(f32[1]{0:T(128)} %bitcast.17, f32[1]{0:T(128)} %bitcast.16), channel_id=1, replica_groups=mesh['row'=4,'col'=16,'layer'=4] {'row','col'}, use_global_device_ids=true, to_apply=%region_7.8 | all-reduce | flops 2 | bytes 16 | tf_op jit(solution)/shard_map/psum | solution.py:81
  507.6 1.8 pad_maximum_fusion
  (7 shorter events, 0.1 us)
Async XLA Ops:
  7.2 48.6 %all-gather.3.cloned.1.call-start = ((), (), s32[]{:S(2)}) async-start(), calls=%async_computation.4 | async-start | bytes 4456448 | tf_op jit(solution)/shard_map/all_gather | solution.py:45
  9.5 104.6 %all-reduce.6.cloned.1.call-start = ((), (), s32[]{:S(2)}) async-start(), calls=%async_computation.5 | async-start | bytes 2097152 | tf_op jit(solution)/shard_map/psum | solution.py:26
  30.0 84.2 %copy-start.3 = (s32[64,64]{1,0:T(8,128)S(1)}, s32[64,64]{1,0:T(8,128)}, u32[]{:S(2)}) copy-start(s32[64,64]{1,0:T(8,128)} %param.3) | copy-start | bytes 49156
  65.6 128.0 %all-reduce.8.cloned.1.call-start = ((), (), s32[]{:S(2)}) async-start(), calls=%async_computation.6 | async-start | bytes 2097152 | tf_op jit(solution)/shard_map/psum | solution.py:26
  134.2 59.4 %copy-start.2 = (f32[1024,256]{1,0:T(8,128)S(1)}, f32[1024,256]{1,0:T(8,128)}, u32[]{:S(2)}) copy-start(f32[1024,256]{1,0:T(8,128)} %all-reduce.6.cloned.1.call-done) | copy-start | bytes 3145732
  144.2 96.2 %all-gather.5.cloned.1.call-start = ((), (), s32[]{:S(2)}) async-start(), calls=%async_computation.7 | async-start | bytes 4456448 | tf_op jit(solution)/shard_map/all_gather | solution.py:45
  196.1 102.6 %all-reduce.10.cloned.1.call-start = ((), (), s32[]{:S(2)}) async-start(), calls=%async_computation.8 | async-start | bytes 2097152 | tf_op jit(solution)/shard_map/psum | solution.py:26
  250.2 125.6 %all-reduce.12.cloned.1.call-start = ((), (), s32[]{:S(2)}) async-start(), calls=%async_computation.9 | async-start | bytes 2097152 | tf_op jit(solution)/shard_map/psum | solution.py:26
  298.8 19.8 %copy-start = (f32[1024,1024]{0,1:T(8,128)S(1)}, f32[1024,1024]{0,1:T(8,128)}, u32[]{:S(2)}) copy-start(f32[1024,1024]{0,1:T(8,128)} %all-gather.5.cloned.1.call-done) | copy-start | bytes 12582916
  318.5 57.3 %copy-start.1 = (f32[1024,256]{1,0:T(8,128)S(1)}, f32[1024,256]{1,0:T(8,128)}, u32[]{:S(2)}) copy-start(f32[1024,256]{1,0:T(8,128)} %all-reduce.10.cloned.1.call-done) | copy-start | bytes 3145732
Sparse Core Ops, SparseCore 0:
  10.4 45.3 all-gather.2
  65.7 48.3 all-reduce.5
  144.3 49.2 all-reduce.7
  196.3 44.0 all-gather.4
  250.3 48.3 all-reduce.9
  326.5 49.2 all-reduce.11
